TPU v7x, 512 devices: a whole 4x8x8 slice. The times are simulated.
512 devices in a mesh: gal: 64 (over x, z, core), pix: 8 (over y).
Axes of the slice: x: 4, y: 8, z: 8, core: 2. Of those that a mesh axis runs over, the one named last changes fastest.
Arguments:
- spectra: bfloat16 [32768, 8192], P('gal', 'pix'), may hold values from -500 to 500
- sketch: bfloat16 [32768, 128], P('gal'), may hold values from -0.25 to 0.25
- block_mask: int32 [64, 64], P('gal', 'pix'), may hold values from 0 to 1, as said below
- rank_key: int32 [64], P('gal'), may hold values from 0 to 63, each once
Outputs:
- projector_basis: float32 [8192, 128], P('pix')
- scores: float32 [32768, 128], P('gal')
Inputs may be any that keep to these rules, and one draw needn't show every extreme that they name: `block_mask`: in every galaxy batch at least half of the 64 blocks are valid.
All inputs are finite; a program needn't handle non-finite values.
Results may differ from a plain program's by a relative error of at most 0.0059.
Values sent between devices are 32-bit elements; how exact they have to be, the bound alone decides.
No kernel may reach another device: no remote copies, remote signals or barrier semaphores. Data moves between devices by JAX's collectives and lax.ppermute only.
A program may use at most 64 MiB of HBM per device.

v0:
```python
import math

import jax
import jax.numpy as jnp
from jax import lax
from jax.sharding import PartitionSpec as P

NPIX = 8192
K = 128
ITERS = 2


def swapped(block, axis, bit):
    count = lax.axis_size(axis)
    route = []
    for low in range(count):
        high = low | 1 << bit
        if high != low and high < count:
            route += [(low, high), (high, low)]
    return lax.ppermute(block, axis, route)


def gram_of(left_side, right_side):
    return lax.dot_general(
        left_side,
        right_side,
        (((0,), (0,)), ((), ())),
        precision=lax.Precision.HIGHEST,
        preferred_element_type=jnp.float32,
    )


def matmul_high(left_side, right_side):
    return jnp.dot(
        left_side, right_side, precision=lax.Precision.HIGHEST, preferred_element_type=jnp.float32
    )


def orthonormal(columns, gram_matrix):
    lower_factor = jnp.linalg.cholesky(gram_matrix)
    return lax.linalg.triangular_solve(
        lower_factor, columns, left_side=False, lower=True, transpose_a=True
    )


def rotate(gram_matrix):
    rotation = jnp.concatenate(
        [jnp.eye(K, dtype=jnp.float32), jnp.zeros((K, K), jnp.float32)], axis=0
    )
    for iteration in range(ITERS):
        mapped = matmul_high(gram_matrix, rotation)
        rotation = orthonormal(mapped, gram_of(mapped, mapped))
    return rotation


def per_device(spectra, sketch, block_mask, rank_key):
    pixel_width = spectra.shape[1]
    pixel_mask = jnp.repeat(block_mask[0], pixel_width // block_mask.shape[1]).astype(jnp.bfloat16)
    masked = spectra * pixel_mask[None, :]
    sketched = lax.dot_general(
        masked, sketch, (((0,), (0,)), ((), ())), preferred_element_type=jnp.float32
    )
    gram_sum = lax.psum(gram_of(sketched, sketched), "pix")
    ortho_panel = orthonormal(sketched, gram_sum)
    ortho_half = ortho_panel.astype(jnp.bfloat16)
    projected = lax.psum(jnp.dot(masked, ortho_half, preferred_element_type=jnp.float32), "pix")
    covariance = gram_of(projected, projected)
    factor = jnp.linalg.cholesky(covariance)
    panel_now = matmul_high(ortho_panel, factor)
    own_gram = gram_of(factor, factor)
    all_keys = lax.all_gather(rank_key, "gal", axis=0, tiled=True)
    position = lax.axis_index("gal")
    level_count = lax.axis_size("gal").bit_length() - 1
    for section in range(level_count):
        block_span = 2**section
        group_min = jnp.min(all_keys.reshape(-1, block_span), axis=1)
        my_group = position // block_span
        own_min = group_min[my_group]
        other_min = group_min[jnp.bitwise_xor(my_group, 1)]
        lead_flag = own_min < other_min
        partner = swapped(panel_now, "gal", section)
        front_panel = jnp.where(lead_flag, panel_now, partner)
        back_panel = jnp.where(lead_flag, partner, panel_now)
        joined = jnp.concatenate([front_panel, back_panel], axis=1)
        gram_matrix = lax.psum(gram_of(joined, joined), "pix")
        rotation = rotate(gram_matrix)
        panel_now = matmul_high(joined, rotation)
        own_gram = gram_of(rotation, matmul_high(gram_matrix, rotation))
    projector_basis = orthonormal(panel_now, own_gram) * math.sqrt(NPIX)
    basis_half = projector_basis.astype(jnp.bfloat16)
    score_terms = jnp.dot(masked, basis_half, preferred_element_type=jnp.float32)
    scores = lax.psum(score_terms, "pix") / NPIX
    return (projector_basis, scores)


def solution(mesh):
    in_specs = (P("gal", "pix"), P("gal", None), P("gal", "pix"), P("gal"))
    out_specs = (P("pix", None), P("gal", None))
    return jax.shard_map(
        per_device, mesh=mesh, in_specs=in_specs, out_specs=out_specs, check_vma=False
    )
```

profile of v0, /device:TPU:6, one launch (start us, length us, event | category | flops | bytes accessed | tf_op | source)
XLA Modules:
  0.0 1212.3 jit_solution(16196803938518872094)
XLA Ops:
  11.5 81.2 %all-reduce.12.cloned.1.call-done = f32[128,128]{0,1:T(8,128)} async-done(((f32[128,128]{0,1:T(8,128)}), f32[128,128]{0,1:T(8,128)}) %all-reduce.12.cloned.1.call-update) | async-done | bytes 65552 | tf_op jit(solution)/shard_map/psum | solution.py:63
  94.5 11.7 cholesky.239
  119.4 76.4 %all-reduce.14.cloned.1.call-done = f32[512,128]{1,0:T(8,128)} async-done(((f32[512,128]{1,0:T(8,128)}), f32[512,128]{1,0:T(8,128)}) %all-reduce.14.cloned.1.call-update) | async-done | bytes 262160 | tf_op jit(solution)/shard_map/psum | solution.py:66
  197.6 11.7 cholesky.250
  215.8 19.7 %all-reduce.1 = s32[64]{0:T(128)S(1)} all-reduce(s32[64]{0:T(128)S(1)} %dynamic-update-slice.2), channel_id=1, replica_groups=mesh['gal'=64,'pix'=8] {'gal'}, use_global_device_ids=true, to_apply=%add.1 | all-reduce | flops 64 | bytes 512
  239.7 72.7 %all-reduce.16.cloned.1.call-done = f32[256,256]{1,0:T(8,128)} async-done(((f32[256,256]{1,0:T(8,128)}), f32[256,256]{1,0:T(8,128)}) %all-reduce.16.cloned.1.call-update) | async-done | bytes 262160 | tf_op jit(solution)/shard_map/psum | solution.py:85
  314.1 11.7 cholesky.261
  338.2 11.7 cholesky.272
  351.3 21.1 %custom-call.22 = f32[1,128,128]{1,2,0:T(8,128)S(1)} custom-call(f32[1,128,128]{2,1,0:T(8,128)S(1)} %fusion.38), custom_call_target="InvertDiagBlocksLowerTriangular" | custom-call | tf_op jit(solution)/shard_map/triangular_solve/custom-call.2 | solution.py:41
  386.4 76.7 %all-reduce.18.cloned.1.call-done = f32[256,256]{1,0:T(8,128)} async-done(((f32[256,256]{1,0:T(8,128)}), f32[256,256]{1,0:T(8,128)}) %all-reduce.18.cloned.1.call-update) | async-done | bytes 262160 | tf_op jit(solution)/shard_map/psum | solution.py:85
  464.8 11.7 cholesky.283
  488.9 11.7 cholesky.294
  502.0 10.2 custom-call.24
  520.0 16.3 %collective-permute-done.2 = f32[1024,128]{0,1:T(8,128)S(1)} collective-permute-done((f32[1024,128]{0,1:T(8,128)S(1)}, f32[1024,128]{0,1:T(8,128)S(1)}, u32[]{:S(2)}, u32[]{:S(2)}) %collective-permute-start.2) | collective-permute-done | bytes 524320 | tf_op jit(solution)/shard_map/ppermute | solution.py:20
  538.2 76.9 %all-reduce.20.cloned.1.call-done = f32[256,256]{1,0:T(8,128)} async-done(((f32[256,256]{1,0:T(8,128)}), f32[256,256]{1,0:T(8,128)}) %all-reduce.20.cloned.1.call-update) | async-done | bytes 262160 | tf_op jit(solution)/shard_map/psum | solution.py:85
  616.8 11.7 cholesky.305
  640.9 11.7 cholesky.316
  653.9 10.0 custom-call.26
  675.1 15.5 %collective-permute-done.3 = f32[1024,128]{0,1:T(8,128)S(1)} collective-permute-done((f32[1024,128]{0,1:T(8,128)S(1)}, f32[1024,128]{0,1:T(8,128)S(1)}, u32[]{:S(2)}, u32[]{:S(2)}) %collective-permute-start.3) | collective-permute-done | bytes 524320 | tf_op jit(solution)/shard_map/ppermute | solution.py:20
  692.5 77.3 %all-reduce.22.cloned.1.call-done = f32[256,256]{1,0:T(8,128)} async-done(((f32[256,256]{1,0:T(8,128)}), f32[256,256]{1,0:T(8,128)}) %all-reduce.22.cloned.1.call-update) | async-done | bytes 262160 | tf_op jit(solution)/shard_map/psum | solution.py:85
  771.5 11.7 cholesky.327
  795.5 11.7 cholesky.338
  808.6 10.2 custom-call.28
  832.8 76.7 %all-reduce.24.cloned.1.call-done = f32[256,256]{1,0:T(8,128)} async-done(((f32[256,256]{1,0:T(8,128)}), f32[256,256]{1,0:T(8,128)}) %all-reduce.24.cloned.1.call-update) | async-done | bytes 262160 | tf_op jit(solution)/shard_map/psum | solution.py:85
  911.3 11.7 cholesky.349
  935.4 11.7 cholesky.360
  973.9 76.7 %all-reduce.26.cloned.1.call-done = f32[256,256]{1,0:T(8,128)} async-done(((f32[256,256]{1,0:T(8,128)}), f32[256,256]{1,0:T(8,128)}) %all-reduce.26.cloned.1.call-update) | async-done | bytes 262160 | tf_op jit(solution)/shard_map/psum | solution.py:85
  1052.3 11.7 cholesky.371
  1076.4 11.7 cholesky.382
  1089.5 10.0 custom-call.32
  1102.4 11.7 cholesky.393
  1128.1 75.6 %all-reduce.28.cloned.1.call-done = f32[512,128]{1,0:T(8,128)} async-done(((f32[512,128]{1,0:T(8,128)}), f32[512,128]{1,0:T(8,128)}) %all-reduce.28.cloned.1.call-update) | async-done | bytes 262160 | tf_op jit(solution)/shard_map/psum | solution.py:92
  (215 shorter events, 209.6 us)
Async XLA Ops:
  7.2 0.9 copy-start
  7.2 85.5 %all-reduce.12.cloned.1.call-start = ((), (), s32[]{:S(2)}) async-start(), calls=%async_computation | async-start | bytes 131072 | tf_op jit(solution)/shard_map/psum | solution.py:63
  11.4 106.6 %copy-start.1 = (bf16[512,1024]{1,0:T(8,128)(2,1)S(1)}, bf16[512,1024]{1,0:T(8,128)(2,1)}, u32[]{:S(2)}) copy-start(bf16[512,1024]{1,0:T(8,128)(2,1)} %param.9) | copy-start | bytes 3145732
  11.4 184.4 %all-reduce.14.cloned.1.call-start = ((), (), s32[]{:S(2)}) async-start(), calls=%async_computation.1 | async-start | bytes 524288 | tf_op jit(solution)/shard_map/psum | solution.py:66
  119.2 193.3 %all-reduce.16.cloned.1.call-start = ((), (), s32[]{:S(2)}) async-start(), calls=%async_computation.2 | async-start | bytes 524288 | tf_op jit(solution)/shard_map/psum | solution.py:85
  211.2 26.2 %collective-permute-start = (f32[1024,128]{0,1:T(8,128)S(1)}, f32[1024,128]{0,1:T(8,128)S(1)}, u32[]{:S(2)}, u32[]{:S(2)}) collective-permute-start(f32[1024,128]{0,1:T(8,128)S(1)} %fusion.80), channel_id=1, source_target_pairs={{0,8},{8,0},{16,24},{24,16},{32,40},{40,32},{48,56},{56,48},{64,72... | collective-permute-start | bytes 1572872 | tf_op jit(solution)/shard_map/ppermute | solution.py:20
  239.3 223.8 %all-reduce.18.cloned.1.call-start = ((), (), s32[]{:S(2)}) async-start(), calls=%async_computation.3 | async-start | bytes 524288 | tf_op jit(solution)/shard_map/psum | solution.py:85
  325.9 11.5 copy-start.3
  373.4 11.1 collective-permute-start.1
  386.4 228.7 %all-reduce.20.cloned.1.call-start = ((), (), s32[]{:S(2)}) async-start(), calls=%async_computation.4 | async-start | bytes 524288 | tf_op jit(solution)/shard_map/psum | solution.py:85
  476.5 11.5 copy-start.4
  513.2 23.1 %collective-permute-start.2 = (f32[1024,128]{0,1:T(8,128)S(1)}, f32[1024,128]{0,1:T(8,128)S(1)}, u32[]{:S(2)}, u32[]{:S(2)}) collective-permute-start(f32[1024,128]{0,1:T(8,128)S(1)} %fusion.9), channel_id=1, source_target_pairs={{0,32},{32,0},{8,40},{40,8},{16,48},{48,16},{24,56},{56,24},{64,96... | collective-permute-start | bytes 1572872 | tf_op jit(solution)/shard_map/ppermute | solution.py:20
  538.2 231.6 %all-reduce.22.cloned.1.call-start = ((), (), s32[]{:S(2)}) async-start(), calls=%async_computation.5 | async-start | bytes 524288 | tf_op jit(solution)/shard_map/psum | solution.py:85
  628.5 11.5 copy-start.5
  664.9 25.6 %collective-permute-start.3 = (f32[1024,128]{0,1:T(8,128)S(1)}, f32[1024,128]{0,1:T(8,128)S(1)}, u32[]{:S(2)}, u32[]{:S(2)}) collective-permute-start(f32[1024,128]{0,1:T(8,128)S(1)} %fusion.7), channel_id=1, source_target_pairs={{0,64},{64,0},{8,72},{72,8},{16,80},{80,16},{24,88},{88,24},{32,96... | collective-permute-start | bytes 1572872 | tf_op jit(solution)/shard_map/ppermute | solution.py:20
  692.4 217.1 %all-reduce.24.cloned.1.call-start = ((), (), s32[]{:S(2)}) async-start(), calls=%async_computation.6 | async-start | bytes 524288 | tf_op jit(solution)/shard_map/psum | solution.py:85
  783.2 11.5 copy-start.6
  819.8 11.1 collective-permute-start.4
  832.8 217.9 %all-reduce.26.cloned.1.call-start = ((), (), s32[]{:S(2)}) async-start(), calls=%async_computation.7 | async-start | bytes 524288 | tf_op jit(solution)/shard_map/psum | solution.py:85
  923.0 11.5 copy-start.7
  959.4 12.6 %collective-permute-start.5 = (f32[1024,128]{0,1:T(8,128)S(1)}, f32[1024,128]{0,1:T(8,128)S(1)}, u32[]{:S(2)}, u32[]{:S(2)}) collective-permute-start(f32[1024,128]{0,1:T(8,128)S(1)} %fusion.3), channel_id=1, source_target_pairs={{0,256},{256,0},{8,264},{264,8},{16,272},{272,16},{24,280},{280,24... | collective-permute-start | bytes 1572872 | tf_op jit(solution)/shard_map/ppermute | solution.py:20
  973.8 229.8 %all-reduce.28.cloned.1.call-start = ((), (), s32[]{:S(2)}) async-start(), calls=%async_computation.8 | async-start | bytes 524288 | tf_op jit(solution)/shard_map/psum | solution.py:92
  1064.1 11.5 copy-start.2
Sparse Core Ops, SparseCore 0:
  11.6 81.0 all-reduce.11
  119.3 76.4 all-reduce.13
  239.5 72.9 all-reduce.15
  386.5 76.5 all-reduce.17
  538.3 76.7 all-reduce.19
  692.5 77.1 all-reduce.21
  832.9 76.6 all-reduce.23
  974.0 76.6 all-reduce.25
  1127.2 76.4 all-reduce.27
where the time goes:
time: 1220 us; the launch traced here: 1210 us
  waiting for transfers between devices  741 us (61%)
  other arithmetic  349 us (29%)
  matrix products  44 us (4%)
  starting transfers between devices  25.1 us (2%)
  between operations  23.8 us (2%)
  blocking collectives  19.7 us (2%)
    psum x6, waiting for transfers between devices, per_device(): gram_matrix = lax.psum(gram_of(joined, joined), 'pix')  457 us
    another operation x43, other arithmetic, orthonormal(): lower_factor = jnp.linalg.cholesky(gram_matrix)  173 us
    another operation x28, other arithmetic, orthonormal(): lax.linalg.triangular_solve(lower_factor, columns, left_side=False, lower...  159 us
    psum x1, waiting for transfers between devices, per_device(): gram_sum = lax.psum(gram_of(sketched, sketched), 'pix')  81.2 us
    psum x1, waiting for transfers between devices, per_device(): lax.psum(jnp.dot(masked, ortho_half, preferred_element_type=jnp.float32),...  76.4 us
    psum x1, waiting for transfers between devices, per_device(): scores = lax.psum(score_terms, 'pix') / NPIX  75.6 us
    ppermute x6, waiting for transfers between devices, swapped(): return lax.ppermute(block, axis, route)  50.4 us
  transfers between devices with their start and end apart: 15, of which 14 were waited for; matrix products, arithmetic and copies ran while one was open for 1% of the time, Pallas kernels for 0%

commit v1 on v0

v1 whole, which is shorter than its diff:
```python
import functools
import math

import jax
import jax.numpy as jnp
from jax import lax
from jax.experimental import pallas as pl
from jax.experimental.pallas import tpu as pltpu
from jax.sharding import PartitionSpec as P

NPIX = 8192
K = 128
PIX = 8
HIGH = lax.Precision.HIGHEST
PARAMS = pltpu.CompilerParams(vmem_limit_bytes=32 * 1024 * 1024)
NB = 32


def dot_of(a, b, dims):
    return lax.dot_general(
        a, b, (dims, ((), ())), precision=HIGH, preferred_element_type=jnp.float32
    )


def nn(a, b):
    return dot_of(a, b, ((1,), (0,)))


def nt(a, b):
    return dot_of(a, b, ((1,), (1,)))


def tn(a, b):
    return dot_of(a, b, ((0,), (0,)))


def split3(x):
    high = x.astype(jnp.bfloat16)
    rest = x - high.astype(jnp.float32)
    middle = rest.astype(jnp.bfloat16)
    low = (rest - middle.astype(jnp.float32)).astype(jnp.bfloat16)
    return high, middle, low


def tn_thin(a, b):
    ah, am, al = split3(a)
    bh, bm, bl = split3(b)
    left = jnp.concatenate([ah, ah, am, am, ah, al], axis=0)
    right = jnp.concatenate([bh, bm, bh, bm, bl, bh], axis=0)
    return lax.dot_general(
        left, right, (((0,), (0,)), ((), ())), preferred_element_type=jnp.float32
    )


def eliminate(work):
    row_id = lax.broadcasted_iota(jnp.int32, (NB, 1), 0)
    for start in range(0, K, NB):
        rows = work[start : start + NB, :]
        for step in range(NB):
            at = start + step
            pivot_row = rows[step : step + 1, :]
            inverse = lax.rsqrt(pivot_row[:, at : at + 1])
            scaled = pivot_row * inverse
            if step < NB - 1:
                column = jnp.where(row_id > step, rows[:, at : at + 1] * inverse, 0.0)
                rows = jnp.where(row_id == step, scaled, rows - column * scaled)
            else:
                rows = jnp.where(row_id == step, scaled, rows)
        work[start : start + NB, :] = rows
        if start + NB < K:
            work[start + NB :, :] = work[start + NB :, :] - tn_thin(
                rows[:, start + NB : K], rows
            )


def leaf_kernel(parts, sketched, out, work_z, work_h):
    rows = sketched.shape[0]
    work_h[...] = jnp.sum(parts[:, :K, :], axis=0)
    for part in range(PIX):
        work_z[16 * part : 16 * (part + 1), :K] = parts[part, K:, :]
    row_at = lax.broadcasted_iota(jnp.int32, (K, K), 0)
    col_at = lax.broadcasted_iota(jnp.int32, (K, K), 1)
    work_z[:, K:] = jnp.where(row_at == col_at, 1.0, 0.0)
    eliminate(work_z)
    eliminate(work_h)
    inverse = work_z[:, K:]
    factor = nt(inverse, jnp.where(col_at >= row_at, work_h[...], 0.0))
    out[:rows, :] = nn(sketched[...], tn(inverse, factor))
    out[rows : rows + K, :] = tn(factor, factor)


def merge_kernel(last, parts, front, back, out, gram, work):
    rows = front.shape[0] - K - 8
    cross = jnp.sum(parts[...], axis=0)
    front_gram = front[rows : rows + K, :]
    back_gram = back[rows : rows + K, :]
    largest = jnp.maximum(
        jnp.max(front_gram, keepdims=True), jnp.max(back_gram, keepdims=True)
    )
    scale = 1.0 / largest
    gram[:K, :K] = front_gram * scale
    gram[:K, K:] = cross * scale
    gram[K:, :K] = cross.T * scale
    gram[K:, K:] = back_gram * scale
    powered = nn(gram[:K, :], gram[...])
    if last:
        work[:, :K] = nt(nn(powered, gram[...]), powered)
    else:
        work[:, :K] = nt(powered, powered)
    work[:, K:] = powered
    eliminate(work)
    rotation = work[:, K:]
    panel = nt(front[:rows, :], rotation[:, :K]) + nt(back[:rows, :], rotation[:, K:])
    if last:
        out[...] = panel * (math.sqrt(NPIX) * jnp.sqrt(scale))
    else:
        out[:rows, :] = panel
        out[rows : rows + K, :] = nt(nn(rotation, gram[...]), rotation) * largest
        out[rows + K :, :] = jnp.minimum(front[rows + K :, :], back[rows + K :, :])


def swapped(block, axis, bit):
    count = lax.axis_size(axis)
    return lax.ppermute(block, axis, [(low, low ^ 1 << bit) for low in range(count)])


def spread(block):
    many = jnp.broadcast_to(block[None], (PIX,) + block.shape)
    return lax.all_to_all(many, "pix", 0, 0)


def per_device(spectra, sketch, block_mask, rank_key):
    batch, width = spectra.shape
    share = batch // PIX
    pixel_mask = jnp.repeat(block_mask[0], width // block_mask.shape[1]).astype(jnp.bfloat16)
    masked = spectra * pixel_mask[None, :]
    sketched = lax.dot_general(
        masked, sketch, (((0,), (0,)), ((), ())), preferred_element_type=jnp.float32
    )
    sketch_gram = tn(sketched, sketched)
    high = sketched.astype(jnp.bfloat16)
    low = (sketched - high.astype(jnp.float32)).astype(jnp.bfloat16)
    both = jnp.dot(
        masked, jnp.concatenate([high, low], axis=1), preferred_element_type=jnp.float32
    )
    projected = both[:, :K] + both[:, K:]
    sends = jnp.concatenate(
        [projected.reshape(PIX, share, K), sketch_gram.reshape(PIX, K // PIX, K)], axis=1
    )
    summed = jnp.sum(lax.all_to_all(sends, "pix", 0, 0), axis=0)
    own_rows = summed[:share]
    parts = spread(jnp.concatenate([tn(own_rows, own_rows), summed[share:]], axis=0))
    state = pl.pallas_call(
        leaf_kernel,
        out_shape=jax.ShapeDtypeStruct((width + K, K), jnp.float32),
        scratch_shapes=[pltpu.VMEM((K, 2 * K), jnp.float32), pltpu.VMEM((K, K), jnp.float32)],
        compiler_params=PARAMS,
        name="leaf",
    )(parts, sketched)
    key_rows = jnp.broadcast_to(rank_key.astype(jnp.float32)[:, None], (8, K))
    state = jnp.concatenate([state, key_rows], axis=0)
    level_count = lax.axis_size("gal").bit_length() - 1
    for level in range(level_count):
        last = level == level_count - 1
        partner = swapped(state, "gal", level)
        lead_flag = state[width + K, 0] < partner[width + K, 0]
        front = jnp.where(lead_flag, state, partner)
        back = jnp.where(lead_flag, partner, state)
        parts = spread(tn(front[:width], back[:width]))
        out_rows = width if last else width + K + 8
        state = pl.pallas_call(
            functools.partial(merge_kernel, last),
            out_shape=jax.ShapeDtypeStruct((out_rows, K), jnp.float32),
            scratch_shapes=[
                pltpu.VMEM((2 * K, 2 * K), jnp.float32),
                pltpu.VMEM((K, 3 * K), jnp.float32),
            ],
            compiler_params=PARAMS,
            name="finish" if last else "merge",
        )(parts, front, back)
    basis_half = state.astype(jnp.bfloat16)
    score_terms = jnp.dot(masked, basis_half, preferred_element_type=jnp.float32)
    own_scores = jnp.sum(
        lax.all_to_all(score_terms.reshape(PIX, share, K), "pix", 0, 0), axis=0
    )
    scores = spread(own_scores * (1.0 / NPIX)).reshape(batch, K)
    return (state, scores)


def solution(mesh):
    in_specs = (P("gal", "pix"), P("gal", None), P("gal", "pix"), P("gal"))
    out_specs = (P("pix", None), P("gal", None))
    return jax.shard_map(
        per_device, mesh=mesh, in_specs=in_specs, out_specs=out_specs, check_vma=False
    )
```

time: 1220 us -> 425 us (0.35)
  waiting for transfers between devices: 741 us -> 99 us
  other arithmetic: 349 us -> 1.28 us
  blocking collectives: 19.7 us -> 164 us
  Pallas kernels: 0 us -> 95.9 us
  matrix products: 44 us -> 10.6 us
  between operations: 23.8 us -> 9.01 us
    psum x9 -> x0, waiting for transfers between devices: 690 us -> none  [the longest x6 457 us: per_device(): gram_matrix = lax.psum(gram_of(joined, joined), 'pix')]
    another operation x74 -> x0, other arithmetic: 345 us -> none  [the longest x43 173 us: orthonormal(): lower_factor = jnp.linalg.cholesky(gram_matrix)]
    all_to_all x0 -> x9, blocking collectives: none -> 164 us  [the longest x7 131 us: spread(): return lax.all_to_all(many, 'pix', 0, 0)]
    pallas_call x0 -> x7, Pallas kernels: none -> 95.9 us  [the longest x6 80.5 us: per_device(): pl.pallas_call(functools.partial(merge_kernel, last), out_shape=jax.Shape...]
    ppermute x6, waiting for transfers between devices: 50.4 us -> 82.7 us  [swapped(): lax.ppermute(block, axis, [(low, low ^ 1 << bit) for low in range(count)])]
    dot_general x42 -> x9, matrix products: 36.2 us -> 7.49 us  [the longest x8 7.02 us: dot_of(): lax.dot_general(a, b, (dims, ((), ())), precision=HIGH, preferred_element...]
    unnamed x1 -> x0, blocking collectives: 19.7 us -> none
    all_to_all x0 -> x1, waiting for transfers between devices: none -> 16.3 us  [spread(): return lax.all_to_all(many, 'pix', 0, 0)]
  transfers between devices with their start and end apart: 15 -> 7, of which waited for: 14 -> 7; matrix products, arithmetic and copies ran while one was open for 1% -> 1% of each run, Pallas kernels for 0% -> 0%
where the time goes in v1:
time: 425 us; the launch traced here: 417 us
  blocking collectives  164 us (39%)
  waiting for transfers between devices  99 us (23%)
  Pallas kernels  95.9 us (23%)
  starting transfers between devices  30.1 us (7%)
  matrix products  10.6 us (2%)
  between operations  9.01 us (2%)
  local copies, waits for them, and re-layouts  7.88 us (2%)
    all_to_all x7, blocking collectives, spread(): return lax.all_to_all(many, 'pix', 0, 0)  131 us
    ppermute x6, waiting for transfers between devices, swapped(): lax.ppermute(block, axis, [(low, low ^ 1 << bit) for low in range(count)])  82.7 us
    pallas_call x6, Pallas kernels, per_device(): pl.pallas_call(functools.partial(merge_kernel, last), out_shape=jax.Shape...  80.5 us
    ppermute x6, starting transfers between devices, swapped(): lax.ppermute(block, axis, [(low, low ^ 1 << bit) for low in range(count)])  26.5 us
    all_to_all x1, blocking collectives, per_device(): summed = jnp.sum(lax.all_to_all(sends, 'pix', 0, 0), axis=0)  20.2 us
    all_to_all x1, waiting for transfers between devices, spread(): return lax.all_to_all(many, 'pix', 0, 0)  16.3 us
    pallas_call x1, Pallas kernels, per_device(): pl.pallas_call(leaf_kernel, out_shape=jax.ShapeDtypeStruct((width + K, K)...  15.4 us
    all_to_all x1, blocking collectives, per_device(): lax.all_to_all(score_terms.reshape(PIX, share, K), 'pix', 0, 0)  12.9 us
  transfers between devices with their start and end apart: 7, of which 7 were waited for; matrix products, arithmetic and copies ran while one was open for 1% of the time, Pallas kernels for 0%

profile of v1, /device:TPU:6, one launch (start us, length us, event | category | flops | bytes accessed | tf_op | source)
XLA Modules:
  0.0 417.4 jit_solution(15098186673524967453)
XLA Ops:
  1.6 1.7 subtract_convert_fusion
  4.4 20.2 %all_to_all.50 = f32[8,80,128]{2,1,0:T(8,128)S(1)} all-to-all(f32[8,80,128]{2,1,0:T(8,128)S(1)} %pad_maximum_fusion), channel_id=1, replica_groups=mesh['gal'=64,'pix'=8] {'pix'}, dimensions={0} | all-to-all | bytes 655360 | tf_op jit(solution)/shard_map/all_to_all | solution.py:150
  25.8 3.5 all-to-all-start.1
  30.2 16.3 %all-to-all-done.1.parts = f32[8,144,128]{2,1,0:T(8,128)S(1)} async-done(((f32[8,144,128]{2,1,0:T(8,128)}), f32[8,144,128]{2,1,0:T(8,128)S(1)}, u32[]{:S(2)}, u32[]{:S(2)}) %all-to-all-start.1) | async-done | bytes 589856 | tf_op jit(solution)/shard_map/all_to_all | solution.py:129
  46.5 15.4 %leaf.1 = f32[1152,128]{1,0:T(8,128)S(1)} custom-call(f32[8,144,128]{2,1,0:T(8,128)S(1)} %all-to-all-done.1.parts, f32[1024,128]{1,0:T(8,128)S(1)} %copy.6.sketched), custom_call_target="tpu_custom_call" | custom-call | tf_op jit(solution)/shard_map/leaf/pallas_call | solution.py:153
  61.9 1.9 collective-permute-start
  63.9 2.0 collective-permute-done
  68.2 20.9 %all_to_all.51.parts = f32[8,128,128]{2,1,0:T(8,128)S(1)} all-to-all(f32[8,128,128]{2,1,0:T(8,128)S(1)} %broadcast_in_dim.23), channel_id=1, replica_groups=mesh['gal'=64,'pix'=8] {'pix'}, dimensions={0} | all-to-all | bytes 1048576 | tf_op jit(solution)/shard_map/all_to_all | solution.py:129
  89.1 13.3 %merge.5 = f32[1160,128]{1,0:T(8,128)S(1)} custom-call(f32[8,128,128]{2,1,0:T(8,128)S(1)} %all_to_all.51.parts, f32[1160,128]{1,0:T(8,128)S(1)} %get-tuple-element.14.front, f32[1160,128]{1,0:T(8,128)S(1)} %get-tuple-element.15.back), custom_call_target="tpu_custom_call" | custom-call | tf_op jit(solution)/shard_map/merge/pallas_call | solution.py:171
  102.4 4.3 %collective-permute-start.1 = (f32[1160,128]{1,0:T(8,128)S(1)}, f32[1160,128]{1,0:T(8,128)S(1)}, u32[]{:S(2)}, u32[]{:S(2)}) collective-permute-start(f32[1160,128]{1,0:T(8,128)S(1)} %merge.5), channel_id=1, source_target_pairs={{0,16},{8,24},{16,0},{24,8},{32,48},{40,56},{48,32},{56,40},{64,80... | collective-permute-start | bytes 1781768 | tf_op jit(solution)/shard_map/ppermute | solution.py:124
  107.2 13.1 %collective-permute-done.1 = f32[1160,128]{1,0:T(8,128)S(1)} collective-permute-done((f32[1160,128]{1,0:T(8,128)S(1)}, f32[1160,128]{1,0:T(8,128)S(1)}, u32[]{:S(2)}, u32[]{:S(2)}) %collective-permute-start.1) | collective-permute-done | bytes 593952 | tf_op jit(solution)/shard_map/ppermute | solution.py:124
  123.3 19.9 %all_to_all.52.parts = f32[8,128,128]{2,1,0:T(8,128)S(1)} all-to-all(f32[8,128,128]{2,1,0:T(8,128)S(1)} %broadcast_in_dim.24), channel_id=1, replica_groups=mesh['gal'=64,'pix'=8] {'pix'}, dimensions={0} | all-to-all | bytes 1048576 | tf_op jit(solution)/shard_map/all_to_all | solution.py:129
  143.1 13.3 %merge.6 = f32[1160,128]{1,0:T(8,128)S(1)} custom-call(f32[8,128,128]{2,1,0:T(8,128)S(1)} %all_to_all.52.parts, f32[1160,128]{1,0:T(8,128)S(1)} %get-tuple-element.12.front, f32[1160,128]{1,0:T(8,128)S(1)} %get-tuple-element.13.back), custom_call_target="tpu_custom_call" | custom-call | tf_op jit(solution)/shard_map/merge/pallas_call | solution.py:171
  156.4 6.1 %collective-permute-start.2 = (f32[1160,128]{1,0:T(8,128)S(1)}, f32[1160,128]{1,0:T(8,128)S(1)}, u32[]{:S(2)}, u32[]{:S(2)}) collective-permute-start(f32[1160,128]{1,0:T(8,128)S(1)} %merge.6), channel_id=1, source_target_pairs={{0,32},{8,40},{16,48},{24,56},{32,0},{40,8},{48,16},{56,24},{64,96... | collective-permute-start | bytes 1781768 | tf_op jit(solution)/shard_map/ppermute | solution.py:124
  163.0 23.7 %collective-permute-done.2 = f32[1160,128]{1,0:T(8,128)S(1)} collective-permute-done((f32[1160,128]{1,0:T(8,128)S(1)}, f32[1160,128]{1,0:T(8,128)S(1)}, u32[]{:S(2)}, u32[]{:S(2)}) %collective-permute-start.2) | collective-permute-done | bytes 593952 | tf_op jit(solution)/shard_map/ppermute | solution.py:124
  189.7 20.4 %all_to_all.53.parts = f32[8,128,128]{2,1,0:T(8,128)S(1)} all-to-all(f32[8,128,128]{2,1,0:T(8,128)S(1)} %broadcast_in_dim.25), channel_id=1, replica_groups=mesh['gal'=64,'pix'=8] {'pix'}, dimensions={0} | all-to-all | bytes 1048576 | tf_op jit(solution)/shard_map/all_to_all | solution.py:129
  210.1 13.3 %merge.7 = f32[1160,128]{1,0:T(8,128)S(1)} custom-call(f32[8,128,128]{2,1,0:T(8,128)S(1)} %all_to_all.53.parts, f32[1160,128]{1,0:T(8,128)S(1)} %get-tuple-element.10.front, f32[1160,128]{1,0:T(8,128)S(1)} %get-tuple-element.11.back), custom_call_target="tpu_custom_call" | custom-call | tf_op jit(solution)/shard_map/merge/pallas_call | solution.py:171
  223.4 7.8 %collective-permute-start.3 = (f32[1160,128]{1,0:T(8,128)S(1)}, f32[1160,128]{1,0:T(8,128)S(1)}, u32[]{:S(2)}, u32[]{:S(2)}) collective-permute-start(f32[1160,128]{1,0:T(8,128)S(1)} %merge.7), channel_id=1, source_target_pairs={{0,64},{8,72},{16,80},{24,88},{32,96},{40,104},{48,112},{56,120},{... | collective-permute-start | bytes 1781768 | tf_op jit(solution)/shard_map/ppermute | solution.py:124
  231.7 23.6 %collective-permute-done.3 = f32[1160,128]{1,0:T(8,128)S(1)} collective-permute-done((f32[1160,128]{1,0:T(8,128)S(1)}, f32[1160,128]{1,0:T(8,128)S(1)}, u32[]{:S(2)}, u32[]{:S(2)}) %collective-permute-start.3) | collective-permute-done | bytes 593952 | tf_op jit(solution)/shard_map/ppermute | solution.py:124
  258.2 19.0 %all_to_all.54.parts = f32[8,128,128]{2,1,0:T(8,128)S(1)} all-to-all(f32[8,128,128]{2,1,0:T(8,128)S(1)} %broadcast_in_dim.26), channel_id=1, replica_groups=mesh['gal'=64,'pix'=8] {'pix'}, dimensions={0} | all-to-all | bytes 1048576 | tf_op jit(solution)/shard_map/all_to_all | solution.py:129
  277.2 13.3 %merge.8 = f32[1160,128]{1,0:T(8,128)S(1)} custom-call(f32[8,128,128]{2,1,0:T(8,128)S(1)} %all_to_all.54.parts, f32[1160,128]{1,0:T(8,128)S(1)} %get-tuple-element.8.front, f32[1160,128]{1,0:T(8,128)S(1)} %get-tuple-element.9.back), custom_call_target="tpu_custom_call" | custom-call | tf_op jit(solution)/shard_map/merge/pallas_call | solution.py:171
  290.5 2.8 collective-permute-start.4
  293.8 10.3 %collective-permute-done.4 = f32[1160,128]{1,0:T(8,128)S(1)} collective-permute-done((f32[1160,128]{1,0:T(8,128)S(1)}, f32[1160,128]{1,0:T(8,128)S(1)}, u32[]{:S(2)}, u32[]{:S(2)}) %collective-permute-start.4) | collective-permute-done | bytes 593952 | tf_op jit(solution)/shard_map/ppermute | solution.py:124
  307.2 18.8 %all_to_all.55.parts = f32[8,128,128]{2,1,0:T(8,128)S(1)} all-to-all(f32[8,128,128]{2,1,0:T(8,128)S(1)} %broadcast_in_dim.27), channel_id=1, replica_groups=mesh['gal'=64,'pix'=8] {'pix'}, dimensions={0} | all-to-all | bytes 1048576 | tf_op jit(solution)/shard_map/all_to_all | solution.py:129
  326.0 13.3 %merge.9 = f32[1160,128]{1,0:T(8,128)S(1)} custom-call(f32[8,128,128]{2,1,0:T(8,128)S(1)} %all_to_all.55.parts, f32[1160,128]{1,0:T(8,128)S(1)} %get-tuple-element.6.front, f32[1160,128]{1,0:T(8,128)S(1)} %get-tuple-element.7.back), custom_call_target="tpu_custom_call" | custom-call | tf_op jit(solution)/shard_map/merge/pallas_call | solution.py:171
  339.3 3.6 collective-permute-start.5
  343.4 10.0 %collective-permute-done.5 = f32[1160,128]{1,0:T(8,128)S(1)} collective-permute-done((f32[1160,128]{1,0:T(8,128)S(1)}, f32[1160,128]{1,0:T(8,128)S(1)}, u32[]{:S(2)}, u32[]{:S(2)}) %collective-permute-start.5) | collective-permute-done | bytes 593952 | tf_op jit(solution)/shard_map/ppermute | solution.py:124
  356.4 18.7 %all_to_all.56.parts = f32[8,128,128]{2,1,0:T(8,128)S(1)} all-to-all(f32[8,128,128]{2,1,0:T(8,128)S(1)} %broadcast_in_dim.28), channel_id=1, replica_groups=mesh['gal'=64,'pix'=8] {'pix'}, dimensions={0} | all-to-all | bytes 1048576 | tf_op jit(solution)/shard_map/all_to_all | solution.py:129
  375.1 14.1 %finish.1 = f32[1024,128]{1,0:T(8,128)} custom-call(f32[8,128,128]{2,1,0:T(8,128)S(1)} %all_to_all.56.parts, f32[1160,128]{1,0:T(8,128)S(1)} %get-tuple-element.4.front, f32[1160,128]{1,0:T(8,128)S(1)} %get-tuple-element.5.back), custom_call_target="tpu_custom_call" | custom-call | tf_op jit(solution)/shard_map/finish/pallas_call | solution.py:171
  389.2 1.5 fusion
  390.7 12.9 %all_to_all.57 = f32[8,64,128]{2,1,0:T(8,128)S(1)} all-to-all(f32[8,64,128]{2,1,0:T(8,128)S(1)} %bitcast.20), channel_id=1, replica_groups=mesh['gal'=64,'pix'=8] {'pix'}, dimensions={0} | all-to-all | bytes 524288 | tf_op jit(solution)/shard_map/all_to_all | solution.py:184
  403.6 12.9 %all_to_all.58 = f32[8,64,128]{2,1,0:T(8,128)S(1)} all-to-all(f32[8,64,128]{2,1,0:T(8,128)S(1)} %broadcast_in_dim.29), channel_id=1, replica_groups=mesh['gal'=64,'pix'=8] {'pix'}, dimensions={0} | all-to-all | bytes 524288 | tf_op jit(solution)/shard_map/all_to_all | solution.py:129
  (50 shorter events, 16.7 us)
Async XLA Ops:
  0.6 0.9 copy-start
  1.6 1.7 copy-start.1
  25.8 20.7 %all-to-all-start.1 = ((f32[8,144,128]{2,1,0:T(8,128)}), f32[8,144,128]{2,1,0:T(8,128)S(1)}, u32[]{:S(2)}, u32[]{:S(2)}) async-start(f32[8,144,128]{2,1,0:T(8,128)} %broadcast_in_dim.22), calls=%async_computation.1 | async-start | bytes 1179648 | tf_op jit(solution)/shard_map/all_to_all | solution.py:129
  61.9 3.9 collective-permute-start
  102.4 17.9 %collective-permute-start.1 = (f32[1160,128]{1,0:T(8,128)S(1)}, f32[1160,128]{1,0:T(8,128)S(1)}, u32[]{:S(2)}, u32[]{:S(2)}) collective-permute-start(f32[1160,128]{1,0:T(8,128)S(1)} %merge.5), channel_id=1, source_target_pairs={{0,16},{8,24},{16,0},{24,8},{32,48},{40,56},{48,32},{56,40},{64,80... | collective-permute-start | bytes 1781768 | tf_op jit(solution)/shard_map/ppermute | solution.py:124
  156.4 30.3 %collective-permute-start.2 = (f32[1160,128]{1,0:T(8,128)S(1)}, f32[1160,128]{1,0:T(8,128)S(1)}, u32[]{:S(2)}, u32[]{:S(2)}) collective-permute-start(f32[1160,128]{1,0:T(8,128)S(1)} %merge.6), channel_id=1, source_target_pairs={{0,32},{8,40},{16,48},{24,56},{32,0},{40,8},{48,16},{56,24},{64,96... | collective-permute-start | bytes 1781768 | tf_op jit(solution)/shard_map/ppermute | solution.py:124
  223.4 31.8 %collective-permute-start.3 = (f32[1160,128]{1,0:T(8,128)S(1)}, f32[1160,128]{1,0:T(8,128)S(1)}, u32[]{:S(2)}, u32[]{:S(2)}) collective-permute-start(f32[1160,128]{1,0:T(8,128)S(1)} %merge.7), channel_id=1, source_target_pairs={{0,64},{8,72},{16,80},{24,88},{32,96},{40,104},{48,112},{56,120},{... | collective-permute-start | bytes 1781768 | tf_op jit(solution)/shard_map/ppermute | solution.py:124
  290.5 13.7 %collective-permute-start.4 = (f32[1160,128]{1,0:T(8,128)S(1)}, f32[1160,128]{1,0:T(8,128)S(1)}, u32[]{:S(2)}, u32[]{:S(2)}) collective-permute-start(f32[1160,128]{1,0:T(8,128)S(1)} %merge.8), channel_id=1, source_target_pairs={{0,128},{8,136},{16,144},{24,152},{32,160},{40,168},{48,176},{56,1... | collective-permute-start | bytes 1781768 | tf_op jit(solution)/shard_map/ppermute | solution.py:124
  339.3 14.1 %collective-permute-start.5 = (f32[1160,128]{1,0:T(8,128)S(1)}, f32[1160,128]{1,0:T(8,128)S(1)}, u32[]{:S(2)}, u32[]{:S(2)}) collective-permute-start(f32[1160,128]{1,0:T(8,128)S(1)} %merge.9), channel_id=1, source_target_pairs={{0,256},{8,264},{16,272},{24,280},{32,288},{40,296},{48,304},{56,3... | collective-permute-start | bytes 1781768 | tf_op jit(solution)/shard_map/ppermute | solution.py:124

commit v2 on v1

v2 whole, which is shorter than its diff:
```python
import functools
import math

import jax
import jax.numpy as jnp
from jax import lax
from jax.experimental import pallas as pl
from jax.experimental.pallas import tpu as pltpu
from jax.sharding import PartitionSpec as P

NPIX = 8192
K = 128
PIX = 8
HIGH = lax.Precision.HIGHEST
PARAMS = pltpu.CompilerParams(vmem_limit_bytes=32 * 1024 * 1024)
NB = 32
LANES = 128


def dot_of(a, b, dims):
    return lax.dot_general(
        a, b, (dims, ((), ())), precision=HIGH, preferred_element_type=jnp.float32
    )


def nn(a, b):
    return dot_of(a, b, ((1,), (0,)))


def nt(a, b):
    return dot_of(a, b, ((1,), (1,)))


def tn(a, b):
    return dot_of(a, b, ((0,), (0,)))


def split3(x):
    high = x.astype(jnp.bfloat16)
    rest = x - high.astype(jnp.float32)
    middle = rest.astype(jnp.bfloat16)
    low = (rest - middle.astype(jnp.float32)).astype(jnp.bfloat16)
    return high, middle, low


def tn_thin(a, b):
    ah, am, al = split3(a)
    bh, bm, bl = split3(b)
    left = jnp.concatenate([ah, ah, am, am, ah, al], axis=0)
    right = jnp.concatenate([bh, bm, bh, bm, bl, bh], axis=0)
    return lax.dot_general(
        left, right, (((0,), (0,)), ((), ())), preferred_element_type=jnp.float32
    )


def whole(x):
    return jnp.broadcast_to(x, (8, LANES))


def across(x, width):
    return jnp.concatenate([x] * (width // LANES), axis=1)


def eliminate_rows(work, at):
    width = work.shape[1]
    end = (at // NB + 1) * NB
    count = (end - at) // 8 - 1
    sub = lax.broadcasted_iota(jnp.int32, (8, width), 0)
    pivots = [jnp.broadcast_to(work[at + i : at + i + 1, :K], (8, K)) for i in range(8)]
    block = [[whole(pivots[i][:, at + k : at + k + 1]) for k in range(i + 1)] for i in range(8)]
    columns = None
    if count:
        columns = [
            jnp.broadcast_to(work[at + 8 : end, at + k : at + k + 1], (8 * count, LANES)).reshape(
                count, 8, LANES
            )
            for k in range(8)
        ]
    lower, scaled_rows, multipliers = [], [], []
    result = None
    for j in range(8):
        inverse = lax.rsqrt(block[j][j])
        factors = [block[i][j] * inverse if i > j else None for i in range(8)]
        for k in range(j + 1, 8):
            for i in range(k, 8):
                block[i][k] = block[i][k] - factors[i] * factors[k]
        if count:
            multiplier = columns[j] * inverse[None]
            for k in range(j + 1, 8):
                columns[k] = columns[k] - multiplier * factors[k][None]
            multipliers.append(multiplier)
        row = jnp.broadcast_to(work[at + j : at + j + 1, :], (8, width))
        for q in range(j):
            row = row - across(lower[q][j], width) * scaled_rows[q]
        row = row * across(inverse, width)
        lower.append(factors)
        scaled_rows.append(row)
        result = row if result is None else jnp.where(sub >= j, row, result)
    work[at : at + 8, :] = result
    for t in range(count):
        rows = work[at + 8 + 8 * t : at + 16 + 8 * t, :]
        for j in range(8):
            rows = rows - across(multipliers[j][t], width) * scaled_rows[j]
        work[at + 8 + 8 * t : at + 16 + 8 * t, :] = rows
    if at + 8 == end and end < K:
        group = work[end - NB : end, :]
        work[end:, :] = work[end:, :] - tn_thin(group[:, end:K], group)


def eliminate(*works):
    for at in range(0, K, 8):
        for work in works:
            eliminate_rows(work, at)


def leaf_kernel(parts, sketched, panel, gram, work_z, work_h):
    work_h[...] = jnp.sum(parts[:, :K, :], axis=0)
    for part in range(PIX):
        work_z[16 * part : 16 * (part + 1), :K] = parts[part, K:, :]
    row_at = lax.broadcasted_iota(jnp.int32, (K, K), 0)
    col_at = lax.broadcasted_iota(jnp.int32, (K, K), 1)
    work_z[:, K:] = jnp.where(row_at == col_at, 1.0, 0.0)
    eliminate(work_z, work_h)
    inverse = work_z[:, K:]
    factor = nt(inverse, jnp.where(col_at >= row_at, work_h[...], 0.0))
    panel[...] = nn(sketched[...], tn(inverse, factor))
    gram[...] = tn(factor, factor)


def merge_kernel(last, core, keys, mine, other, own_gram, partner_gram, front, back, *refs):
    out, gram, work = refs[0], refs[-2], refs[-1]
    rows = front.shape[0]
    half = K // 2
    second = core[:1, :] > 0.5
    lead = keys[:1, :] < keys[8:9, :]
    top = jnp.where(second, other[...], mine[...])
    low = jnp.where(second, mine[...], other[...])
    front_gram = jnp.where(lead, own_gram[...], partner_gram[...])
    back_gram = jnp.where(lead, partner_gram[...], own_gram[...])
    largest = jnp.maximum(
        jnp.max(front_gram, keepdims=True), jnp.max(back_gram, keepdims=True)
    )
    scale = 1.0 / largest
    gram[:K, :K] = front_gram * scale
    gram[:half, K:] = top * scale
    gram[half:K, K:] = low * scale
    gram[K:, :K] = gram[:K, K:].T
    gram[K:, K:] = back_gram * scale
    powered = nn(gram[:K, :], gram[...])
    if last:
        work[:, :K] = nt(nn(powered, gram[...]), powered)
    else:
        work[:, :K] = nt(powered, powered)
    work[:, K:] = powered
    eliminate(work)
    rotation = work[:, K:]
    panel = nt(front[...], rotation[:, :K]) + nt(back[...], rotation[:, K:])
    if last:
        out[...] = panel * (math.sqrt(NPIX) * jnp.sqrt(scale))
    else:
        out[:rows, :] = panel
        merged = nt(nn(rotation, gram[...]), rotation) * largest
        refs[1][...] = merged
        out[rows : rows + half, :] = jnp.where(second, merged[half:, :], merged[:half, :])
        out[rows + half :, :] = jnp.minimum(keys[:8, :], keys[8:, :])


def swapped(block, axis, bit):
    count = lax.axis_size(axis)
    return lax.ppermute(block, axis, [(low, low ^ 1 << bit) for low in range(count)])


def spread(block):
    many = jnp.broadcast_to(block[None], (PIX,) + block.shape)
    return lax.all_to_all(many, "pix", 0, 0)


def per_device(spectra, sketch, block_mask, rank_key):
    batch, width = spectra.shape
    share = batch // PIX
    rows = width // 2
    half = K // 2
    second = lax.axis_index("gal") % 2 == 1
    core_rows = jnp.broadcast_to(second.astype(jnp.float32), (8, K))
    pixel_mask = jnp.repeat(block_mask[0], width // block_mask.shape[1]).astype(jnp.bfloat16)
    masked = spectra * pixel_mask[None, :]
    sketched = lax.dot_general(
        masked, sketch, (((0,), (0,)), ((), ())), preferred_element_type=jnp.float32
    )
    sketch_gram = tn(sketched, sketched)
    high = lax.reduce_precision(sketched, 8, 7)
    low = sketched - high
    pieces = jnp.concatenate([high.astype(jnp.bfloat16), low.astype(jnp.bfloat16)], axis=1)
    both = jnp.dot(masked, pieces, preferred_element_type=jnp.float32)
    projected = both[:, :K] + both[:, K:]
    sends = jnp.concatenate(
        [projected.reshape(PIX, share, K), sketch_gram.reshape(PIX, K // PIX, K)], axis=1
    )
    summed = jnp.sum(lax.all_to_all(sends, "pix", 0, 0), axis=0)
    own_rows = summed[:share]
    parts = spread(jnp.concatenate([tn(own_rows, own_rows), summed[share:]], axis=0))
    leaf_panel, own_gram = pl.pallas_call(
        leaf_kernel,
        out_shape=[
            jax.ShapeDtypeStruct((width, K), jnp.float32),
            jax.ShapeDtypeStruct((K, K), jnp.float32),
        ],
        scratch_shapes=[pltpu.VMEM((K, 2 * K), jnp.float32), pltpu.VMEM((K, K), jnp.float32)],
        compiler_params=PARAMS,
        name="leaf",
    )(parts, sketched)
    key_rows = jnp.broadcast_to(rank_key.astype(jnp.float32)[:, None], (8, K))
    kept = jnp.where(second, leaf_panel[rows:], leaf_panel[:rows])
    sent = jnp.where(second, leaf_panel[:rows], leaf_panel[rows:])
    got = swapped(jnp.concatenate([sent, own_gram, key_rows], axis=0), "gal", 0)
    other_panel, partner_gram, other_key = got[:rows], got[rows : rows + K], got[rows + K :]
    level_count = lax.axis_size("gal").bit_length() - 1
    for level in range(level_count):
        last = level == level_count - 1
        if level:
            got = swapped(state, "gal", level)
            kept, key_rows = state[:rows], state[rows + half :]
            other_panel, other_key = got[:rows], got[rows + half :]
        lead = key_rows[:1] < other_key[:1]
        front = jnp.where(lead, kept, other_panel)
        back = jnp.where(lead, other_panel, kept)
        cross = tn(front, back)
        cross_sent = jnp.where(second, cross[:half], cross[half:])
        cross_kept = jnp.where(second, cross[half:], cross[:half])
        mine = jnp.sum(spread(cross_kept + swapped(cross_sent, "gal", 0)), axis=0)
        if level:
            gram_half = got[rows : rows + half]
            other = swapped(jnp.concatenate([mine, gram_half], axis=0), "gal", 0)
            other, other_half = other[:half], other[half:]
            partner_gram = jnp.concatenate(
                [
                    jnp.where(second, other_half, gram_half),
                    jnp.where(second, gram_half, other_half),
                ],
                axis=0,
            )
        else:
            other = swapped(mine, "gal", 0)
        keys = jnp.concatenate([key_rows, other_key], axis=0)
        if last:
            out_shape = jax.ShapeDtypeStruct((rows, K), jnp.float32)
        else:
            out_shape = [
                jax.ShapeDtypeStruct((rows + half + 8, K), jnp.float32),
                jax.ShapeDtypeStruct((K, K), jnp.float32),
            ]
        state = pl.pallas_call(
            functools.partial(merge_kernel, last),
            out_shape=out_shape,
            scratch_shapes=[
                pltpu.VMEM((2 * K, 2 * K), jnp.float32),
                pltpu.VMEM((K, 3 * K), jnp.float32),
            ],
            compiler_params=PARAMS,
            name="finish" if last else "merge",
        )(core_rows, keys, mine, other, own_gram, partner_gram, front, back)
        if not last:
            state, own_gram = state
    other = swapped(state, "gal", 0)
    basis = jnp.concatenate(
        [jnp.where(second, other, state), jnp.where(second, state, other)], axis=0
    )
    score_terms = jnp.dot(masked, basis.astype(jnp.bfloat16), preferred_element_type=jnp.float32)
    own_scores = jnp.sum(
        lax.all_to_all(score_terms.reshape(PIX, share, K), "pix", 0, 0), axis=0
    )
    scores = spread(own_scores * (1.0 / NPIX)).reshape(batch, K)
    return (basis, scores)


def solution(mesh):
    in_specs = (P("gal", "pix"), P("gal", None), P("gal", "pix"), P("gal"))
    out_specs = (P("pix", None), P("gal", None))
    return jax.shard_map(
        per_device, mesh=mesh, in_specs=in_specs, out_specs=out_specs, check_vma=False
    )
```

time: 425 us -> 341 us (0.80); the launches traced: 417 us -> 338 us
  blocking collectives: 164 us -> 64.7 us
  Pallas kernels: 95.9 us -> 35.7 us
  waiting for transfers between devices: 99 us -> 146 us
  starting transfers between devices: 30.1 us -> 73.7 us
  between operations: 9.01 us -> 2.29 us
    all_to_all x7 -> x2, blocking collectives: 131 us -> 29.7 us  [spread(): return lax.all_to_all(many, 'pix', 0, 0)]
    all_to_all x1 -> x6, waiting for transfers between devices: 16.3 us -> 78.1 us  [spread(): return lax.all_to_all(many, 'pix', 0, 0)]
    pallas_call x7, Pallas kernels: 95.9 us -> 35.7 us  [the longest x6 29.7 us: per_device(): pl.pallas_call(functools.partial(merge_kernel, last), out_shape=out_shape...]
    ppermute x6 -> x19, starting transfers between devices: 26.5 us -> 53.1 us  [swapped(): lax.ppermute(block, axis, [(low, low ^ 1 << bit) for low in range(count)])]
    all_to_all x1 -> x6, starting transfers between devices: 3.54 us -> 20.6 us  [spread(): return lax.all_to_all(many, 'pix', 0, 0)]
    ppermute x6 -> x19, waiting for transfers between devices: 82.7 us -> 68.4 us  [swapped(): lax.ppermute(block, axis, [(low, low ^ 1 << bit) for low in range(count)])]
    slice x11 -> x27, local copies, waits for them, and re-layouts: 5.64 us -> 0.09 us  [the longest x10 0.03 us: per_device(): gram_half = got[rows:rows + half]]
  transfers between devices with their start and end apart: 7 -> 25, of which waited for: 7 -> 25; matrix products, arithmetic and copies ran while one was open for 1% -> 0% of each run, Pallas kernels for 0% -> 0%
where the time goes in v2:
time: 341 us; the launch traced here: 338 us
  waiting for transfers between devices  146 us (43%)
  starting transfers between devices  73.7 us (22%)
  blocking collectives  64.7 us (19%)
  Pallas kernels  35.7 us (10%)
  matrix products  6.89 us (2%)
  local copies, waits for them, and re-layouts  6.79 us (2%)
    all_to_all x6, waiting for transfers between devices, spread(): return lax.all_to_all(many, 'pix', 0, 0)  78.1 us
    ppermute x19, waiting for transfers between devices, swapped(): lax.ppermute(block, axis, [(low, low ^ 1 << bit) for low in range(count)])  68.4 us
    ppermute x19, starting transfers between devices, swapped(): lax.ppermute(block, axis, [(low, low ^ 1 << bit) for low in range(count)])  53.1 us
    pallas_call x6, Pallas kernels, per_device(): pl.pallas_call(functools.partial(merge_kernel, last), out_shape=out_shape...  29.7 us
    all_to_all x2, blocking collectives, spread(): return lax.all_to_all(many, 'pix', 0, 0)  29.7 us
    all_to_all x6, starting transfers between devices, spread(): return lax.all_to_all(many, 'pix', 0, 0)  20.6 us
    all_to_all x1, blocking collectives, per_device(): summed = jnp.sum(lax.all_to_all(sends, 'pix', 0, 0), axis=0)  20.2 us
    all_to_all x1, blocking collectives, per_device(): lax.all_to_all(score_terms.reshape(PIX, share, K), 'pix', 0, 0)  14.9 us
  transfers between devices with their start and end apart: 25, of which 25 were waited for; matrix products, arithmetic and copies ran while one was open for 0% of the time, Pallas kernels for 0%

profile of v2, /device:TPU:6, one launch (start us, length us, event | category | flops | bytes accessed | tf_op | source)
XLA Modules:
  0.0 338.1 jit_solution(14794320552318616081)
XLA Ops:
  4.9 20.2 %all_to_all.50 = f32[8,80,128]{2,1,0:T(8,128)S(1)} all-to-all(f32[8,80,128]{2,1,0:T(8,128)S(1)} %pad_maximum_fusion.1), channel_id=1, replica_groups=mesh['gal'=64,'pix'=8] {'pix'}, dimensions={0} | all-to-all | bytes 655360 | tf_op jit(solution)/shard_map/all_to_all | solution.py:199
  26.3 3.5 %all-to-all-start.1 = ((f32[8,144,128]{2,1,0:T(8,128)}), f32[8,144,128]{2,1,0:T(8,128)S(1)}, u32[]{:S(2)}, u32[]{:S(2)}) async-start(f32[8,144,128]{2,1,0:T(8,128)} %broadcast_in_dim.128), calls=%async_computation.1 | async-start | bytes 1179648 | tf_op jit(solution)/shard_map/all_to_all | solution.py:175
  30.8 16.3 %all-to-all-done.1.parts = f32[8,144,128]{2,1,0:T(8,128)S(1)} async-done(((f32[8,144,128]{2,1,0:T(8,128)}), f32[8,144,128]{2,1,0:T(8,128)S(1)}, u32[]{:S(2)}, u32[]{:S(2)}) %all-to-all-start.1) | async-done | bytes 589856 | tf_op jit(solution)/shard_map/all_to_all | solution.py:175
  47.1 5.9 %leaf.1 = (f32[1024,128]{1,0:T(8,128)S(1)}, f32[128,128]{1,0:T(8,128)S(1)}) custom-call(f32[8,144,128]{2,1,0:T(8,128)S(1)} %all-to-all-done.1.parts, f32[1024,128]{1,0:T(8,128)S(1)} %copy.7.sketched), custom_call_target="tpu_custom_call" | custom-call | tf_op jit(solution)/shard_map/leaf/pallas_call | solution.py:202
  60.5 14.9 %all_to_all.51 = f32[8,64,128]{2,1,0:T(8,128)S(1)} all-to-all(f32[8,64,128]{2,1,0:T(8,128)S(1)} %broadcast_in_dim.133), channel_id=1, replica_groups=mesh['gal'=64,'pix'=8] {'pix'}, dimensions={0} | all-to-all | bytes 524288 | tf_op jit(solution)/shard_map/all_to_all | solution.py:175
  78.5 4.9 %merge.5 = (f32[584,128]{1,0:T(8,128)S(1)}, f32[128,128]{1,0:T(8,128)S(1)}) custom-call(f32[8,128]{1,0:T(8,128)S(1)} %broadcast_in_dim.126.core, f32[16,128]{1,0:T(8,128)S(1)} %concatenate.67.keys, f32[64,128]{1,0:T(8,128)S(1)} %reduce_sum.73.mine, f32[64,128]{1,0:T(8,128)S(1)} %collective-permute-done.2.other, f32[128,128]{1,0:T(8,128)S(1)} %get-tuple-element.15.own_gram, ...), custom_call_target="tpu_custom_call" | custom-call | tf_op jit(solution)/shard_map/merge/pallas_call | solution.py:252
  83.5 4.5 %collective-permute-start.3 = (f32[584,128]{1,0:T(8,128)S(1)}, f32[584,128]{1,0:T(8,128)S(1)}, u32[]{:S(2)}, u32[]{:S(2)}) collective-permute-start(f32[584,128]{1,0:T(8,128)S(1)} %get-tuple-element.16), channel_id=1, source_target_pairs={{0,16},{8,24},{16,0},{24,8},{32,48},{40,56},{48,32},{56,40},{64,80... | collective-permute-start | bytes 897032 | tf_op jit(solution)/shard_map/ppermute | solution.py:170
  88.0 7.2 %collective-permute-done.3 = f32[584,128]{1,0:T(8,128)S(1)} collective-permute-done((f32[584,128]{1,0:T(8,128)S(1)}, f32[584,128]{1,0:T(8,128)S(1)}, u32[]{:S(2)}, u32[]{:S(2)}) %collective-permute-start.3) | collective-permute-done | bytes 299040 | tf_op jit(solution)/shard_map/ppermute | solution.py:170
  99.7 3.4 %all-to-all-start.3 = ((f32[8,64,128]{2,1,0:T(8,128)}), f32[8,64,128]{2,1,0:T(8,128)S(1)}, u32[]{:S(2)}, u32[]{:S(2)}) async-start(f32[8,64,128]{2,1,0:T(8,128)} %broadcast_in_dim.136), calls=%async_computation.3 | async-start | bytes 524288 | tf_op jit(solution)/shard_map/all_to_all | solution.py:175
  103.2 12.4 %all-to-all-done.3 = f32[8,64,128]{2,1,0:T(8,128)S(1)} async-done(((f32[8,64,128]{2,1,0:T(8,128)}), f32[8,64,128]{2,1,0:T(8,128)S(1)}, u32[]{:S(2)}, u32[]{:S(2)}) %all-to-all-start.3) | async-done | bytes 262176 | tf_op jit(solution)/shard_map/all_to_all | solution.py:175
  118.8 5.0 %merge.6 = (f32[584,128]{1,0:T(8,128)S(1)}, f32[128,128]{1,0:T(8,128)S(1)}) custom-call(f32[8,128]{1,0:T(8,128)S(1)} %broadcast_in_dim.126.core, f32[16,128]{1,0:T(8,128)S(1)} %pad_maximum_fusion.13.keys, f32[64,128]{1,0:T(8,128)S(1)} %reduce_sum.74.mine, f32[64,128]{1,0:T(8,128)S(1)} %get-tuple-element.56.other, f32[128,128]{1,0:T(8,128)S(1)} %get-tuple-element.17.own_gram, ...), custom_call_target="tpu_custom_call" | custom-call | tf_op jit(solution)/shard_map/merge/pallas_call | solution.py:252
  123.7 6.1 %collective-permute-start.6 = (f32[584,128]{1,0:T(8,128)S(1)}, f32[584,128]{1,0:T(8,128)S(1)}, u32[]{:S(2)}, u32[]{:S(2)}) collective-permute-start(f32[584,128]{1,0:T(8,128)S(1)} %get-tuple-element.18), channel_id=1, source_target_pairs={{0,32},{8,40},{16,48},{24,56},{32,0},{40,8},{48,16},{56,24},{64,96... | collective-permute-start | bytes 897032 | tf_op jit(solution)/shard_map/ppermute | solution.py:170
  129.8 13.8 %collective-permute-done.6 = f32[584,128]{1,0:T(8,128)S(1)} collective-permute-done((f32[584,128]{1,0:T(8,128)S(1)}, f32[584,128]{1,0:T(8,128)S(1)}, u32[]{:S(2)}, u32[]{:S(2)}) %collective-permute-start.6) | collective-permute-done | bytes 299040 | tf_op jit(solution)/shard_map/ppermute | solution.py:170
  148.1 3.4 %all-to-all-start.4 = ((f32[8,64,128]{2,1,0:T(8,128)}), f32[8,64,128]{2,1,0:T(8,128)S(1)}, u32[]{:S(2)}, u32[]{:S(2)}) async-start(f32[8,64,128]{2,1,0:T(8,128)} %broadcast_in_dim.139), calls=%async_computation.4 | async-start | bytes 524288 | tf_op jit(solution)/shard_map/all_to_all | solution.py:175
  151.6 12.4 %all-to-all-done.4 = f32[8,64,128]{2,1,0:T(8,128)S(1)} async-done(((f32[8,64,128]{2,1,0:T(8,128)}), f32[8,64,128]{2,1,0:T(8,128)S(1)}, u32[]{:S(2)}, u32[]{:S(2)}) %all-to-all-start.4) | async-done | bytes 262176 | tf_op jit(solution)/shard_map/all_to_all | solution.py:175
  167.2 4.9 %merge.7 = (f32[584,128]{1,0:T(8,128)S(1)}, f32[128,128]{1,0:T(8,128)S(1)}) custom-call(f32[8,128]{1,0:T(8,128)S(1)} %broadcast_in_dim.126.core, f32[16,128]{1,0:T(8,128)S(1)} %pad_maximum_fusion.14.keys, f32[64,128]{1,0:T(8,128)S(1)} %reduce_sum.75.mine, f32[64,128]{1,0:T(8,128)S(1)} %get-tuple-element.55.other, f32[128,128]{1,0:T(8,128)S(1)} %get-tuple-element.19.own_gram, ...), custom_call_target="tpu_custom_call" | custom-call | tf_op jit(solution)/shard_map/merge/pallas_call | solution.py:252
  172.1 8.7 %collective-permute-start.9 = (f32[584,128]{1,0:T(8,128)S(1)}, f32[584,128]{1,0:T(8,128)S(1)}, u32[]{:S(2)}, u32[]{:S(2)}) collective-permute-start(f32[584,128]{1,0:T(8,128)S(1)} %get-tuple-element.20), channel_id=1, source_target_pairs={{0,64},{8,72},{16,80},{24,88},{32,96},{40,104},{48,112},{56,120},{... | collective-permute-start | bytes 897032 | tf_op jit(solution)/shard_map/ppermute | solution.py:170
  180.9 13.4 %collective-permute-done.9 = f32[584,128]{1,0:T(8,128)S(1)} collective-permute-done((f32[584,128]{1,0:T(8,128)S(1)}, f32[584,128]{1,0:T(8,128)S(1)}, u32[]{:S(2)}, u32[]{:S(2)}) %collective-permute-start.9) | collective-permute-done | bytes 299040 | tf_op jit(solution)/shard_map/ppermute | solution.py:170
  198.8 3.4 %all-to-all-start.5 = ((f32[8,64,128]{2,1,0:T(8,128)}), f32[8,64,128]{2,1,0:T(8,128)S(1)}, u32[]{:S(2)}, u32[]{:S(2)}) async-start(f32[8,64,128]{2,1,0:T(8,128)} %broadcast_in_dim.142), calls=%async_computation.5 | async-start | bytes 524288 | tf_op jit(solution)/shard_map/all_to_all | solution.py:175
  202.2 12.4 %all-to-all-done.5 = f32[8,64,128]{2,1,0:T(8,128)S(1)} async-done(((f32[8,64,128]{2,1,0:T(8,128)}), f32[8,64,128]{2,1,0:T(8,128)S(1)}, u32[]{:S(2)}, u32[]{:S(2)}) %all-to-all-start.5) | async-done | bytes 262176 | tf_op jit(solution)/shard_map/all_to_all | solution.py:175
  217.8 5.0 %merge.8 = (f32[584,128]{1,0:T(8,128)S(1)}, f32[128,128]{1,0:T(8,128)S(1)}) custom-call(f32[8,128]{1,0:T(8,128)S(1)} %broadcast_in_dim.126.core, f32[16,128]{1,0:T(8,128)S(1)} %pad_maximum_fusion.15.keys, f32[64,128]{1,0:T(8,128)S(1)} %reduce_sum.76.mine, f32[64,128]{1,0:T(8,128)S(1)} %get-tuple-element.54.other, f32[128,128]{1,0:T(8,128)S(1)} %get-tuple-element.21.own_gram, ...), custom_call_target="tpu_custom_call" | custom-call | tf_op jit(solution)/shard_map/merge/pallas_call | solution.py:252
  225.5 8.3 %collective-permute-done.12 = f32[584,128]{1,0:T(8,128)S(1)} collective-permute-done((f32[584,128]{1,0:T(8,128)S(1)}, f32[584,128]{1,0:T(8,128)S(1)}, u32[]{:S(2)}, u32[]{:S(2)}) %collective-permute-start.12) | collective-permute-done | bytes 299040 | tf_op jit(solution)/shard_map/ppermute | solution.py:170
  238.3 3.4 %all-to-all-start.6 = ((f32[8,64,128]{2,1,0:T(8,128)}), f32[8,64,128]{2,1,0:T(8,128)S(1)}, u32[]{:S(2)}, u32[]{:S(2)}) async-start(f32[8,64,128]{2,1,0:T(8,128)} %broadcast_in_dim.145), calls=%async_computation.6 | async-start | bytes 524288 | tf_op jit(solution)/shard_map/all_to_all | solution.py:175
  241.8 12.4 %all-to-all-done.6 = f32[8,64,128]{2,1,0:T(8,128)S(1)} async-done(((f32[8,64,128]{2,1,0:T(8,128)}), f32[8,64,128]{2,1,0:T(8,128)S(1)}, u32[]{:S(2)}, u32[]{:S(2)}) %all-to-all-start.6) | async-done | bytes 262176 | tf_op jit(solution)/shard_map/all_to_all | solution.py:175
  257.4 4.9 %merge.9 = (f32[584,128]{1,0:T(8,128)S(1)}, f32[128,128]{1,0:T(8,128)S(1)}) custom-call(f32[8,128]{1,0:T(8,128)S(1)} %broadcast_in_dim.126.core, f32[16,128]{1,0:T(8,128)S(1)} %pad_maximum_fusion.16.keys, f32[64,128]{1,0:T(8,128)S(1)} %reduce_sum.77.mine, f32[64,128]{1,0:T(8,128)S(1)} %get-tuple-element.53.other, f32[128,128]{1,0:T(8,128)S(1)} %get-tuple-element.23.own_gram, ...), custom_call_target="tpu_custom_call" | custom-call | tf_op jit(solution)/shard_map/merge/pallas_call | solution.py:252
  262.3 3.3 collective-permute-start.15
  265.7 9.2 %collective-permute-done.15 = f32[584,128]{1,0:T(8,128)S(1)} collective-permute-done((f32[584,128]{1,0:T(8,128)S(1)}, f32[584,128]{1,0:T(8,128)S(1)}, u32[]{:S(2)}, u32[]{:S(2)}) %collective-permute-start.15) | collective-permute-done | bytes 299040 | tf_op jit(solution)/shard_map/ppermute | solution.py:170
  279.4 3.4 %all-to-all-start.7 = ((f32[8,64,128]{2,1,0:T(8,128)}), f32[8,64,128]{2,1,0:T(8,128)S(1)}, u32[]{:S(2)}, u32[]{:S(2)}) async-start(f32[8,64,128]{2,1,0:T(8,128)} %broadcast_in_dim.148), calls=%async_computation.7 | async-start | bytes 524288 | tf_op jit(solution)/shard_map/all_to_all | solution.py:175
  282.9 12.4 %all-to-all-done.7 = f32[8,64,128]{2,1,0:T(8,128)S(1)} async-done(((f32[8,64,128]{2,1,0:T(8,128)}), f32[8,64,128]{2,1,0:T(8,128)S(1)}, u32[]{:S(2)}, u32[]{:S(2)}) %all-to-all-start.7) | async-done | bytes 262176 | tf_op jit(solution)/shard_map/all_to_all | solution.py:175
  298.4 5.0 %finish.1 = f32[512,128]{1,0:T(8,128)S(1)} custom-call(f32[8,128]{1,0:T(8,128)S(1)} %broadcast_in_dim.126.core, f32[16,128]{1,0:T(8,128)S(1)} %pad_maximum_fusion.17.keys, f32[64,128]{1,0:T(8,128)S(1)} %reduce_sum.78.mine, f32[64,128]{1,0:T(8,128)S(1)} %get-tuple-element.52.other, f32[128,128]{1,0:T(8,128)S(1)} %get-tuple-element.25.own_gram, ...), custom_call_target="tpu_custom_call" | custom-call | tf_op jit(solution)/shard_map/finish/pallas_call | solution.py:252
  307.7 14.9 %all_to_all.52 = f32[8,64,128]{2,1,0:T(8,128)S(1)} all-to-all(f32[8,64,128]{2,1,0:T(8,128)S(1)} %bitcast.38), channel_id=1, replica_groups=mesh['gal'=64,'pix'=8] {'pix'}, dimensions={0} | all-to-all | bytes 524288 | tf_op jit(solution)/shard_map/all_to_all | solution.py:270
  322.7 14.8 %all_to_all.53 = f32[8,64,128]{2,1,0:T(8,128)S(1)} all-to-all(f32[8,64,128]{2,1,0:T(8,128)S(1)} %broadcast_in_dim.149), channel_id=1, replica_groups=mesh['gal'=64,'pix'=8] {'pix'}, dimensions={0} | all-to-all | bytes 524288 | tf_op jit(solution)/shard_map/all_to_all | solution.py:175
  (170 shorter events, 62.2 us)
Async XLA Ops:
  26.3 20.7 %all-to-all-start.1 = ((f32[8,144,128]{2,1,0:T(8,128)}), f32[8,144,128]{2,1,0:T(8,128)S(1)}, u32[]{:S(2)}, u32[]{:S(2)}) async-start(f32[8,144,128]{2,1,0:T(8,128)} %broadcast_in_dim.128), calls=%async_computation.1 | async-start | bytes 1179648 | tf_op jit(solution)/shard_map/all_to_all | solution.py:175
  53.2 3.5 %collective-permute-start = (f32[648,128]{1,0:T(8,128)S(1)}, f32[648,128]{1,0:T(8,128)S(1)}, u32[]{:S(2)}, u32[]{:S(2)}) collective-permute-start(f32[648,128]{1,0:T(8,128)S(1)} %maximum_maximum_fusion), channel_id=1, source_target_pairs={{0,8},{8,0},{16,24},{24,16},{32,40},{40,32},{48,56},{56,48},{64,72... | collective-permute-start | bytes 995336 | tf_op jit(solution)/shard_map/ppermute | solution.py:170
  57.4 3.1 collective-permute-start.1
  75.4 3.1 collective-permute-start.2
  83.5 11.7 %collective-permute-start.3 = (f32[584,128]{1,0:T(8,128)S(1)}, f32[584,128]{1,0:T(8,128)S(1)}, u32[]{:S(2)}, u32[]{:S(2)}) collective-permute-start(f32[584,128]{1,0:T(8,128)S(1)} %get-tuple-element.16), channel_id=1, source_target_pairs={{0,16},{8,24},{16,0},{24,8},{32,48},{40,56},{48,32},{56,40},{64,80... | collective-permute-start | bytes 897032 | tf_op jit(solution)/shard_map/ppermute | solution.py:170
  95.9 3.1 collective-permute-start.4
  99.7 15.8 %all-to-all-start.3 = ((f32[8,64,128]{2,1,0:T(8,128)}), f32[8,64,128]{2,1,0:T(8,128)S(1)}, u32[]{:S(2)}, u32[]{:S(2)}) async-start(f32[8,64,128]{2,1,0:T(8,128)} %broadcast_in_dim.136), calls=%async_computation.3 | async-start | bytes 524288 | tf_op jit(solution)/shard_map/all_to_all | solution.py:175
  103.2 15.6 %copy-start.4 = (f32[584,128]{1,0:T(8,128)S(1)}, f32[584,128]{1,0:T(8,128)}, u32[]{:S(2)}) copy-start(f32[584,128]{1,0:T(8,128)} %copy-done.3) | copy-start | bytes 897028
  115.6 3.1 collective-permute-start.5
  123.7 19.9 %collective-permute-start.6 = (f32[584,128]{1,0:T(8,128)S(1)}, f32[584,128]{1,0:T(8,128)S(1)}, u32[]{:S(2)}, u32[]{:S(2)}) collective-permute-start(f32[584,128]{1,0:T(8,128)S(1)} %get-tuple-element.18), channel_id=1, source_target_pairs={{0,32},{8,40},{16,48},{24,56},{32,0},{40,8},{48,16},{56,24},{64,96... | collective-permute-start | bytes 897032 | tf_op jit(solution)/shard_map/ppermute | solution.py:170
  144.3 3.1 collective-permute-start.7
  148.1 15.8 %all-to-all-start.4 = ((f32[8,64,128]{2,1,0:T(8,128)}), f32[8,64,128]{2,1,0:T(8,128)S(1)}, u32[]{:S(2)}, u32[]{:S(2)}) async-start(f32[8,64,128]{2,1,0:T(8,128)} %broadcast_in_dim.139), calls=%async_computation.4 | async-start | bytes 524288 | tf_op jit(solution)/shard_map/all_to_all | solution.py:175
  151.5 12.4 %slice-start.3 = ((f32[584,128]{1,0:T(8,128)}), f32[64,128]{1,0:T(8,128)S(1)}, s32[]{:S(2)}) async-start(f32[584,128]{1,0:T(8,128)} %copy-done.5), calls=%async_computation.13 | async-start | bytes 65536 | tf_op jit(solution)/shard_map/slice | solution.py:232
  151.6 15.6 %copy-start.6 = (f32[584,128]{1,0:T(8,128)S(1)}, f32[584,128]{1,0:T(8,128)}, u32[]{:S(2)}) copy-start(f32[584,128]{1,0:T(8,128)} %copy-done.5) | copy-start | bytes 897028
  164.0 3.1 collective-permute-start.8
  172.1 22.2 %collective-permute-start.9 = (f32[584,128]{1,0:T(8,128)S(1)}, f32[584,128]{1,0:T(8,128)S(1)}, u32[]{:S(2)}, u32[]{:S(2)}) collective-permute-start(f32[584,128]{1,0:T(8,128)S(1)} %get-tuple-element.20), channel_id=1, source_target_pairs={{0,64},{8,72},{16,80},{24,88},{32,96},{40,104},{48,112},{56,120},{... | collective-permute-start | bytes 897032 | tf_op jit(solution)/shard_map/ppermute | solution.py:170
  194.9 3.1 collective-permute-start.10
  198.8 15.8 %all-to-all-start.5 = ((f32[8,64,128]{2,1,0:T(8,128)}), f32[8,64,128]{2,1,0:T(8,128)S(1)}, u32[]{:S(2)}, u32[]{:S(2)}) async-start(f32[8,64,128]{2,1,0:T(8,128)} %broadcast_in_dim.142), calls=%async_computation.5 | async-start | bytes 524288 | tf_op jit(solution)/shard_map/all_to_all | solution.py:175
  202.2 12.4 %slice-start.5 = ((f32[584,128]{1,0:T(8,128)}), f32[64,128]{1,0:T(8,128)S(1)}, s32[]{:S(2)}) async-start(f32[584,128]{1,0:T(8,128)} %copy-done.7), calls=%async_computation.15 | async-start | bytes 65536 | tf_op jit(solution)/shard_map/slice | solution.py:232
  202.2 15.6 %copy-start.8 = (f32[584,128]{1,0:T(8,128)S(1)}, f32[584,128]{1,0:T(8,128)}, u32[]{:S(2)}) copy-start(f32[584,128]{1,0:T(8,128)} %copy-done.7) | copy-start | bytes 897028
  214.6 3.1 collective-permute-start.11
  222.8 11.1 %collective-permute-start.12 = (f32[584,128]{1,0:T(8,128)S(1)}, f32[584,128]{1,0:T(8,128)S(1)}, u32[]{:S(2)}, u32[]{:S(2)}) collective-permute-start(f32[584,128]{1,0:T(8,128)S(1)} %get-tuple-element.22), channel_id=1, source_target_pairs={{0,128},{8,136},{16,144},{24,152},{32,160},{40,168},{48,176},{56,1... | collective-permute-start | bytes 897032 | tf_op jit(solution)/shard_map/ppermute | solution.py:170
  234.5 3.1 collective-permute-start.13
  238.3 15.8 %all-to-all-start.6 = ((f32[8,64,128]{2,1,0:T(8,128)}), f32[8,64,128]{2,1,0:T(8,128)S(1)}, u32[]{:S(2)}, u32[]{:S(2)}) async-start(f32[8,64,128]{2,1,0:T(8,128)} %broadcast_in_dim.145), calls=%async_computation.6 | async-start | bytes 524288 | tf_op jit(solution)/shard_map/all_to_all | solution.py:175
  241.8 15.6 %copy-start.10 = (f32[584,128]{1,0:T(8,128)S(1)}, f32[584,128]{1,0:T(8,128)}, u32[]{:S(2)}) copy-start(f32[584,128]{1,0:T(8,128)} %copy-done.9) | copy-start | bytes 897028
  254.2 3.1 collective-permute-start.14
  262.3 12.6 %collective-permute-start.15 = (f32[584,128]{1,0:T(8,128)S(1)}, f32[584,128]{1,0:T(8,128)S(1)}, u32[]{:S(2)}, u32[]{:S(2)}) collective-permute-start(f32[584,128]{1,0:T(8,128)S(1)} %get-tuple-element.24), channel_id=1, source_target_pairs={{0,256},{8,264},{16,272},{24,280},{32,288},{40,296},{48,304},{56,3... | collective-permute-start | bytes 897032 | tf_op jit(solution)/shard_map/ppermute | solution.py:170
  275.6 3.1 collective-permute-start.16
  279.4 15.8 %all-to-all-start.7 = ((f32[8,64,128]{2,1,0:T(8,128)}), f32[8,64,128]{2,1,0:T(8,128)S(1)}, u32[]{:S(2)}, u32[]{:S(2)}) async-start(f32[8,64,128]{2,1,0:T(8,128)} %broadcast_in_dim.148), calls=%async_computation.7 | async-start | bytes 524288 | tf_op jit(solution)/shard_map/all_to_all | solution.py:175
  282.8 15.6 %copy-start.12 = (f32[584,128]{1,0:T(8,128)S(1)}, f32[584,128]{1,0:T(8,128)}, u32[]{:S(2)}) copy-start(f32[584,128]{1,0:T(8,128)} %copy-done.11) | copy-start | bytes 897028
  295.3 3.1 collective-permute-start.17
  303.4 3.4 %collective-permute-start.18 = (f32[512,128]{1,0:T(8,128)S(1)}, f32[512,128]{1,0:T(8,128)S(1)}, u32[]{:S(2)}, u32[]{:S(2)}) collective-permute-start(f32[512,128]{1,0:T(8,128)S(1)} %finish.1), channel_id=1, source_target_pairs={{0,8},{8,0},{16,24},{24,16},{32,40},{40,32},{48,56},{56,48},{64,72... | collective-permute-start | bytes 786440 | tf_op jit(solution)/shard_map/ppermute | solution.py:170
  (16 other events, 90.2 us)
